TPU v7x, 32 devices: a whole 2x2x4 slice. The times are simulated.
32 devices in a mesh: dp: 4 (over y, core), expert: 8 (over z, x).
Axes of the slice: x: 2, y: 2, z: 4, core: 2. Of those that a mesh axis runs over, the one named last changes fastest.
Arguments:
- tokens: bfloat16 [2, 512, 3584], P(None, ('dp', 'expert')), parts along dimension 1, may hold values from -6 to 6
- expert_ids: int32 [2, 512, 2], P(None, ('dp', 'expert')), parts along dimension 1, may hold values from 0 to 3, as said below
- route_weights: float32 [2, 512, 2], P(None, ('dp', 'expert')), parts along dimension 1, may hold values from 0.4 to 2
- owner_map: int32 [16], P('dp'), parts along dimension 0, may hold values from 0 to 3, each once
- expert_weights: bfloat16 [4096, 3, 3584], P('expert'), may hold values from -0.09375 to 0.09375
Outputs:
- mixed: bfloat16 [2, 512, 3584], P(None, ('dp', 'expert')), parts along dimension 1
There are 4 independent parts, one for each index of `dp`. A program takes and returns all parts, laid end to end along the dimension named above; an argument that names none is the same for every part. Nothing has to cross between parts.
Inputs may be any that keep to these rules, and one draw needn't show every extreme that they name: `expert_ids`: each token names 2 different experts. One expert, the same for all steps and devices of a part, is named by at least 8 of the tokens of every device in every step, by all 16 tokens of some device in some step, and by more of the tokens of every device over the 2 steps together than any other expert; every other expert is named by at most 8 tokens of one device in one step, a bound reached in every draw. `owner_map`: each group owns exactly one expert.
All inputs are finite; a program needn't handle non-finite values.
Results may differ from a plain program's by a relative error of at most 0.006.
Values may be sent and summed in bfloat16 or wider, within the bound.
A program may use at most 64 MiB of HBM per device.

v0:
```python
import jax
import jax.numpy as jnp
from jax import lax
from jax.sharding import PartitionSpec as P

EXPERTS = 4


def expert_apply(tok_rows, weights):
    gate_up = jnp.einsum(
        "nd,hgd->ngh", tok_rows, weights[:, :2, :], preferred_element_type=jnp.float32
    )
    hidden = (jax.nn.silu(gate_up[:, 0]) * gate_up[:, 1]).astype(jnp.bfloat16)
    return jnp.dot(hidden, weights[:, 2, :], preferred_element_type=jnp.float32).astype(
        jnp.bfloat16
    )


def cold_path(tok_rows, route_ids, coefficient, owner_map, active, capacity, device_count, weights):
    width = tok_rows.shape[1]
    copies = device_count // EXPERTS
    expert_range = jnp.arange(EXPERTS)
    match_table = route_ids[:, :, None] == expert_range[None, None, :]
    is_named = jnp.any(match_table, axis=1) & active[None, :]
    named_int = is_named.astype(jnp.int32)
    before = jnp.cumsum(named_int, axis=0) - named_int
    owner_table = owner_map[:, None] == expert_range[None, :]
    named_group = jnp.any(is_named[:, :, None] & owner_table[None], axis=1)
    before_group = jnp.sum(jnp.where(owner_table[None], before[:, :, None], 0), axis=1)
    slot_index = jnp.arange(capacity)
    selector = (
        named_group.T[:, None, :] & (before_group.T[:, None, :] == slot_index[None, :, None])
    ).astype(jnp.bfloat16)
    blocks = jnp.einsum(
        "gjn,nd->gjd", selector, tok_rows, preferred_element_type=jnp.float32
    ).astype(jnp.bfloat16)
    outgoing = jnp.broadcast_to(blocks[:, None], (EXPERTS, copies, capacity, width)).reshape(
        device_count, capacity, width
    )
    received = lax.all_to_all(outgoing, "expert", split_axis=0, concat_axis=0, tiled=True)
    item_count = received.shape[1]
    partial_value = expert_apply(received.reshape(-1, width), weights).reshape(
        device_count, item_count, width
    )
    returned = lax.all_to_all(partial_value, "expert", split_axis=0, concat_axis=0, tiled=True)
    summed = jnp.sum(returned.astype(jnp.float32).reshape(EXPERTS, copies, capacity, width), axis=1)
    summed = summed.reshape(EXPERTS * capacity, width)
    group_of = jnp.sum(jnp.where(match_table, owner_map[None, None, :], 0), axis=2)
    slot_of = jnp.sum(jnp.where(match_table, before[:, None, :], 0), axis=2)
    kept = jnp.any(match_table & active[None, None, :], axis=2)
    flat_index = jnp.where(kept, group_of * capacity + slot_of, 0)
    picked = jnp.take(summed, flat_index.reshape(-1), axis=0).reshape(
        route_ids.shape[0], route_ids.shape[1], width
    )
    scaled = jnp.where(kept, coefficient, 0.0)
    return jnp.sum(scaled[:, :, None] * picked, axis=1)


def shards(tokens, expert_ids, route_weights, owner_map, expert_weights):
    device_count = lax.axis_size("expert")
    step_count = tokens.shape[0]
    outputs = []
    expert_range = jnp.arange(EXPERTS)
    active = expert_range >= 0
    for step_index in range(step_count):
        cold_output = cold_path(
            tokens[step_index],
            expert_ids[step_index],
            route_weights[step_index],
            owner_map,
            active,
            tokens.shape[1],
            device_count,
            expert_weights,
        )
        outputs.append(cold_output.astype(jnp.bfloat16))
    return jnp.stack(outputs, axis=0)


def solution(mesh):
    placed = (
        P(None, ("dp", "expert"), None),
        P(None, ("dp", "expert"), None),
        P(None, ("dp", "expert"), None),
        P("dp"),
        P("expert", None, None),
    )
    return jax.shard_map(
        shards,
        mesh=mesh,
        in_specs=placed,
        out_specs=P(None, ("dp", "expert"), None),
        check_vma=False,
    )
```

profile of v0, /device:TPU:0, one launch (start us, length us, event | category | flops | bytes accessed | tf_op | source)
XLA Modules:
  0.0 119.0 jit_solution(5215890021220219472)
XLA Ops:
  0.0 0.0 copy-start.1
  0.0 0.0 copy-start
  0.0 0.7 slice_bitcast_fusion
  0.8 0.1 copy.19
  0.9 0.1 copy.20
  1.0 0.7 iota_compare_fusion.4
  1.7 0.1 copy.24
  1.9 0.1 copy.25
  1.9 0.1 and_reduce_fusion.1
  2.0 0.1 select_reduce_fusion.1
  2.1 1.1 convolution_convert_fusion.2
  3.3 1.0 broadcast_in_dim.129
  4.3 7.3 %all-to-all-start.2 = ((bf16[8,16,3584]{2,1,0:T(8,128)(2,1)}), bf16[8,16,3584]{2,1,0:T(8,128)(2,1)S(1)}, u32[]{:S(2)}, u32[]{:S(2)}) async-start(bf16[8,16,3584]{2,1,0:T(8,128)(2,1)} %bitcast.22), calls=%async_computation.2 | async-start | bytes 1835008 | tf_op jit(solution)/shard_map/all_to_all | solution.py:40
  11.5 1.1 convolution_convert_fusion.3
  12.7 21.9 %all-to-all-done.2 = bf16[8,16,3584]{2,1,0:T(8,128)(2,1)S(1)} async-done(((bf16[8,16,3584]{2,1,0:T(8,128)(2,1)}), bf16[8,16,3584]{2,1,0:T(8,128)(2,1)S(1)}, u32[]{:S(2)}, u32[]{:S(2)}) %all-to-all-start.2) | async-done | bytes 917536 | tf_op jit(solution)/shard_map/all_to_all | solution.py:40
  34.6 1.0 broadcast_in_dim.123
  35.6 3.6 %all-to-all-start = ((bf16[8,16,3584]{2,1,0:T(8,128)(2,1)}), bf16[8,16,3584]{2,1,0:T(8,128)(2,1)S(1)}, u32[]{:S(2)}, u32[]{:S(2)}) async-start(bf16[8,16,3584]{2,1,0:T(8,128)(2,1)} %bitcast.6), calls=%async_computation | async-start | bytes 1835008 | tf_op jit(solution)/shard_map/all_to_all | solution.py:40
  39.1 0.0 copy-done.1
  39.2 0.1 select_reduce_fusion.5
  39.2 0.0 copy-done
  39.3 5.5 %fusion.11 = f32[128,2,512]{2,0,1:T(8,128)S(1)} fusion(bf16[128,3584,1]{1,0,2:T(8,128)(2,1)S(1)} %bitcast.64, bf16[512,3,3584]{2,0,1:T(8,128)(2,1)} %param.11), kind=kOutput, calls=%fused_computation.17 | convolution fusion | flops 939524096 | bytes 8781824 | tf_op jit(solution)/shard_map/nd,hgd->ngh/dot_general | solution.py:10
  44.8 3.6 %convolution_convert_fusion = bf16[128,3584]{1,0:T(8,128)(2,1)} fusion(bf16[512,3,3584]{2,0,1:T(8,128)(2,1)} %param.11, f32[128,2,512]{2,0,1:T(8,128)S(1)} %fusion.11), kind=kOutput, calls=%fused_computation.6 | convolution fusion | flops 470614016 | bytes 5111808 | tf_op jit(solution)/shard_map/dot_general | solution.py:14
  48.4 13.8 %all-to-all-done = bf16[8,16,3584]{2,1,0:T(8,128)(2,1)S(1)} async-done(((bf16[8,16,3584]{2,1,0:T(8,128)(2,1)}), bf16[8,16,3584]{2,1,0:T(8,128)(2,1)S(1)}, u32[]{:S(2)}, u32[]{:S(2)}) %all-to-all-start) | async-done | bytes 917536 | tf_op jit(solution)/shard_map/all_to_all | solution.py:40
  62.2 3.6 %all-to-all-start.3 = ((bf16[8,16,3584]{2,1,0:T(8,128)(2,1)}), bf16[8,16,3584]{2,1,0:T(8,128)(2,1)S(1)}, u32[]{:S(2)}, u32[]{:S(2)}) async-start(bf16[8,16,3584]{2,1,0:T(8,128)(2,1)} %bitcast.27), calls=%async_computation.3 | async-start | bytes 1835008 | tf_op jit(solution)/shard_map/all_to_all | solution.py:45
  65.8 0.1 copy.26
  65.9 0.1 select_n.69
  66.0 0.1 copy.23
  66.1 0.1 copy.21
  66.2 0.1 select_n.63
  66.3 0.1 copy.18
  66.4 5.5 %fusion.8 = f32[128,2,512]{2,0,1:T(8,128)S(1)} fusion(bf16[128,3584,1]{1,0,2:T(8,128)(2,1)S(1)} %bitcast.63, bf16[512,3,3584]{2,0,1:T(8,128)(2,1)} %param.11), kind=kOutput, calls=%fused_computation.16 | convolution fusion | flops 939524096 | bytes 8781824 | tf_op jit(solution)/shard_map/nd,hgd->ngh/dot_general | solution.py:10
  71.9 3.7 %convolution_convert_fusion.1 = bf16[128,3584]{1,0:T(8,128)(2,1)} fusion(bf16[512,3,3584]{2,0,1:T(8,128)(2,1)} %param.11, f32[128,2,512]{2,0,1:T(8,128)S(1)} %fusion.8), kind=kOutput, calls=%fused_computation.7 | convolution fusion | flops 470614016 | bytes 5111808 | tf_op jit(solution)/shard_map/dot_general | solution.py:14
  75.6 13.4 %all-to-all-done.3 = bf16[8,16,3584]{2,1,0:T(8,128)(2,1)S(1)} async-done(((bf16[8,16,3584]{2,1,0:T(8,128)(2,1)}), bf16[8,16,3584]{2,1,0:T(8,128)(2,1)S(1)}, u32[]{:S(2)}, u32[]{:S(2)}) %all-to-all-start.3) | async-done | bytes 917536 | tf_op jit(solution)/shard_map/all_to_all | solution.py:45
  89.0 3.6 %all-to-all-start.1 = ((bf16[8,16,3584]{2,1,0:T(8,128)(2,1)}), bf16[8,16,3584]{2,1,0:T(8,128)(2,1)S(1)}, u32[]{:S(2)}, u32[]{:S(2)}) async-start(bf16[8,16,3584]{2,1,0:T(8,128)(2,1)} %bitcast.12), calls=%async_computation.1 | async-start | bytes 1835008 | tf_op jit(solution)/shard_map/all_to_all | solution.py:45
  92.6 0.1 convert_reduce_fusion
  92.7 0.7 gather_fusion.1
  93.5 0.1 broadcast_select_fusion
  93.6 0.3 reshape.183
  93.8 21.9 %all-to-all-done.1 = bf16[8,16,3584]{2,1,0:T(8,128)(2,1)S(1)} async-done(((bf16[8,16,3584]{2,1,0:T(8,128)(2,1)}), bf16[8,16,3584]{2,1,0:T(8,128)(2,1)S(1)}, u32[]{:S(2)}, u32[]{:S(2)}) %all-to-all-start.1) | async-done | bytes 917536 | tf_op jit(solution)/shard_map/all_to_all | solution.py:45
  115.7 0.1 convert_reduce_fusion.1
  115.8 0.7 gather_fusion
  116.6 0.1 broadcast_select_fusion.1
  116.7 0.3 reshape.176
  116.9 0.6 multiply_reduce_fusion
  117.6 0.6 multiply_reduce_fusion.1
  118.2 0.7 pad_maximum_fusion
  (16 shorter events, 0.2 us)
Async XLA Ops:
  0.0 39.1 %copy-start.1 = (s32[4]{0:T(128)S(1)}, s32[4]{0:T(128)}, u32[]{:S(2)}) copy-start(s32[4]{0:T(128)} %param.10) | copy-start | bytes 52
  0.0 39.2 %copy-start = (f32[2,16,2]{1,2,0:T(2,128)S(1)}, f32[2,16,2]{1,2,0:T(2,128)}, u32[]{:S(2)}) copy-start(f32[2,16,2]{1,2,0:T(2,128)} %param.9) | copy-start | bytes 772
  4.3 30.3 %all-to-all-start.2 = ((bf16[8,16,3584]{2,1,0:T(8,128)(2,1)}), bf16[8,16,3584]{2,1,0:T(8,128)(2,1)S(1)}, u32[]{:S(2)}, u32[]{:S(2)}) async-start(bf16[8,16,3584]{2,1,0:T(8,128)(2,1)} %bitcast.22), calls=%async_computation.2 | async-start | bytes 1835008 | tf_op jit(solution)/shard_map/all_to_all | solution.py:40
  35.6 26.7 %all-to-all-start = ((bf16[8,16,3584]{2,1,0:T(8,128)(2,1)}), bf16[8,16,3584]{2,1,0:T(8,128)(2,1)S(1)}, u32[]{:S(2)}, u32[]{:S(2)}) async-start(bf16[8,16,3584]{2,1,0:T(8,128)(2,1)} %bitcast.6), calls=%async_computation | async-start | bytes 1835008 | tf_op jit(solution)/shard_map/all_to_all | solution.py:40
  62.2 26.7 %all-to-all-start.3 = ((bf16[8,16,3584]{2,1,0:T(8,128)(2,1)}), bf16[8,16,3584]{2,1,0:T(8,128)(2,1)S(1)}, u32[]{:S(2)}, u32[]{:S(2)}) async-start(bf16[8,16,3584]{2,1,0:T(8,128)(2,1)} %bitcast.27), calls=%async_computation.3 | async-start | bytes 1835008 | tf_op jit(solution)/shard_map/all_to_all | solution.py:45
  89.0 26.7 %all-to-all-start.1 = ((bf16[8,16,3584]{2,1,0:T(8,128)(2,1)}), bf16[8,16,3584]{2,1,0:T(8,128)(2,1)S(1)}, u32[]{:S(2)}, u32[]{:S(2)}) async-start(bf16[8,16,3584]{2,1,0:T(8,128)(2,1)} %bitcast.12), calls=%async_computation.1 | async-start | bytes 1835008 | tf_op jit(solution)/shard_map/all_to_all | solution.py:45
where the time goes:
time: 120 us; the launch traced here: 119 us
  waiting for transfers between devices  70.9 us (59%)
  matrix products  20.7 us (17%)
  starting transfers between devices  18 us (15%)
  local copies, waits for them, and re-layouts  5.57 us (5%)
  other arithmetic  3.64 us (3%)
    all_to_all x2, waiting for transfers between devices, cold_path(): lax.all_to_all(outgoing, 'expert', split_axis=0, concat_axis=0, tiled=True)  35.7 us
    all_to_all x2, waiting for transfers between devices, cold_path(): lax.all_to_all(partial_value, 'expert', split_axis=0, concat_axis=0, tile...  35.2 us
    dot_general x2, matrix products, expert_apply(): jnp.einsum('nd,hgd->ngh', tok_rows, weights[:, :2, :], preferred_element_...  11 us
    all_to_all x2, starting transfers between devices, cold_path(): lax.all_to_all(outgoing, 'expert', split_axis=0, concat_axis=0, tiled=True)  10.8 us
    dot_general x2, matrix products, expert_apply(): jnp.dot(hidden, weights[:, 2, :], preferred_element_type=jnp.float32)  7.34 us
    all_to_all x2, starting transfers between devices, cold_path(): lax.all_to_all(partial_value, 'expert', split_axis=0, concat_axis=0, tile...  7.18 us
  transfers between devices with their start and end apart: 4, of which 4 were waited for; matrix products, arithmetic and copies ran while one was open for 18% of the time, Pallas kernels for 0%

commit v1 on v0

v1 whole, which is shorter than its diff:
```python
import functools

import jax
import jax.numpy as jnp
from jax import lax
from jax.experimental import pallas as pl
from jax.experimental.pallas import tpu as pltpu
from jax.sharding import PartitionSpec as P

LANES = 128
PIECES = 2


def kernel(groups, copies, x_ref, ext_ref, w_ref, out_ref, w_buf, got, part, from_minor, joined, from_major,
           w_sem, gs_sem, gr_sem, ms_sem, mr_sem, zs_sem, zr_sem):
    steps, rows, width = x_ref.shape
    units = w_ref.shape[1]
    me = lax.axis_index("expert")
    m, c = me // copies, me % copies
    total_rows = groups * copies * rows
    piece = width // PIECES
    majors = [(m + 1 - 2 * (m % 2)), (m + 2) % groups, groups - 1 - m]
    minors = [(c + j) % copies for j in range(1, copies)]

    loads = [pltpu.make_async_copy(w_ref.at[i], w_buf.at[i], w_sem.at[i]) for i in range(3)]
    for load in loads:
        load.start()
    for s in range(steps):
        got[s, me, :, :width] = x_ref[s]
        got[s, me, :, width:] = ext_ref[s]

    barrier = pltpu.get_barrier_semaphore()
    for mp in majors:
        pl.semaphore_signal(barrier, inc=1, device_id={"expert": mp * copies + c}, device_id_type=pl.DeviceIdType.MESH)
    for cp in minors:
        pl.semaphore_signal(barrier, inc=1, device_id={"expert": m * copies + cp}, device_id_type=pl.DeviceIdType.MESH)
    pl.semaphore_wait(barrier, len(majors) + len(minors))

    sends = []

    def remote(src, dst, send_sem, recv_sem, target):
        return pltpu.make_async_remote_copy(src_ref=src, dst_ref=dst, send_sem=send_sem, recv_sem=recv_sem,
                                            device_id={"expert": target}, device_id_type=pl.DeviceIdType.MESH)

    def gather_major(s, k):
        copy = remote(got.at[s, me], got.at[s, me], gs_sem.at[s, k], gr_sem.at[s, k], majors[k] * copies + c)
        copy.start()
        sends.append(copy)

    def gather_wait_major(s, k):
        slot = got.at[s, majors[k] * copies + c]
        remote(slot, slot, gs_sem.at[s, k], gr_sem.at[s, k], majors[k] * copies + c).wait_recv()

    def route(k, j):
        return len(majors) + (k + 1) * len(minors) + j

    def relay(s, k):
        home = m if k < 0 else majors[k]
        slot = got.at[s, home * copies + c]
        for j, cp in enumerate(minors):
            q = route(k, j)
            copy = remote(slot, slot, gs_sem.at[s, q], gr_sem.at[s, q], m * copies + cp)
            copy.start()
            sends.append(copy)

    def relay_wait(s):
        for k in range(-1, len(majors)):
            home = m if k < 0 else majors[k]
            for j in range(len(minors)):
                q = route(k, j)
                origin = (c + copies - (j + 1)) % copies
                slot = got.at[s, home * copies + origin]
                remote(slot, slot, gs_sem.at[s, q], gr_sem.at[s, q], m * copies + origin).wait_recv()

    def hidden_of(s, between):
        block = min(256, units)
        hs = []
        x = got[s, :, :, :width].reshape(total_rows, width)
        for i in range(units // block):
            cut = pl.ds(i * block, block)
            dims = (((1,), (1,)), ((), ()))
            gate = lax.dot_general(x, w_buf[0, cut, :], dims, preferred_element_type=jnp.float32)
            up = lax.dot_general(x, w_buf[1, cut, :], dims, preferred_element_type=jnp.float32)
            hs.append((jax.nn.silu(gate) * up).astype(jnp.bfloat16))
            if i == 0:
                between()
        return jnp.concatenate(hs, axis=1) if len(hs) > 1 else hs[0]

    def scale_of(s):
        ext = got[s, :, :, width:].reshape(total_rows, LANES).astype(jnp.float32)
        lane = lax.broadcasted_iota(jnp.int32, ext.shape, 1)
        mine = (lane % groups == m) & (lane < 3 * groups)
        return jnp.sum(jnp.where(mine, ext, 0.0), axis=1, keepdims=True)

    def down(s, hidden, scale):
        for p in range(PIECES):
            cut = pl.ds(p * piece, piece)
            y = jnp.dot(hidden, w_buf[2, :, cut], preferred_element_type=jnp.float32)
            part[s, :, :, :, cut] = (y * scale).astype(jnp.bfloat16).reshape(groups, copies, rows, piece)
            for j, cp in enumerate(minors):
                copy = remote(part.at[s, :, cp, :, cut], from_minor.at[s, c, :, :, cut],
                              ms_sem.at[s, p, j], mr_sem.at[s, p, j], m * copies + cp)
                copy.start()
                sends.append(copy)

    def join(s):
        for p in range(PIECES):
            cut = pl.ds(p * piece, piece)
            total = part[s, :, c, :, cut].astype(jnp.float32)
            for j in range(len(minors)):
                origin = (c + copies - (j + 1)) % copies
                landed = from_minor.at[s, origin, :, :, cut]
                remote(landed, landed, ms_sem.at[s, p, j], mr_sem.at[s, p, j], m * copies + origin).wait_recv()
                total += from_minor[s, origin, :, :, cut].astype(jnp.float32)
            joined[s, :, :, cut] = total.astype(jnp.bfloat16)
            for k, mp in enumerate(majors):
                copy = remote(joined.at[s, mp, :, cut], from_major.at[s, m, :, cut],
                              zs_sem.at[s, p, k], zr_sem.at[s, p, k], mp * copies + c)
                copy.start()
                sends.append(copy)

    def finish(s):
        for p in range(PIECES):
            cut = pl.ds(p * piece, piece)
            total = joined[s, m, :, cut].astype(jnp.float32)
            for k, mp in enumerate(majors):
                landed = from_major.at[s, mp, :, cut]
                remote(landed, landed, zs_sem.at[s, p, k], zr_sem.at[s, p, k], mp * copies + c).wait_recv()
                total += from_major[s, mp, :, cut].astype(jnp.float32)
            out_ref[s, :, cut] = total.astype(out_ref.dtype)

    for s in range(steps):
        relay(s, -1)
        for k in range(len(majors)):
            gather_major(s, k)

    def forward(s):
        for k in range(len(majors)):
            gather_wait_major(s, k)
            relay(s, k)

    forward(0)
    for s in range(steps):
        relay_wait(s)
        if s == 0:
            loads[0].wait()
            loads[1].wait()

        def between(s=s):
            if s + 1 < steps:
                forward(s + 1)

        hidden = hidden_of(s, between)
        if s == 0:
            loads[2].wait()
        else:
            join(s - 1)
        down(s, hidden, scale_of(s))
    join(steps - 1)
    for s in range(steps):
        finish(s)
    for copy in sends:
        copy.wait_send()


def shards(tokens, expert_ids, route_weights, owner_map, expert_weights):
    device_count = lax.axis_size("expert")
    groups = owner_map.shape[0]
    copies = device_count // groups
    steps, rows, width = tokens.shape
    units = expert_weights.shape[0]
    weights = jnp.transpose(expert_weights, (1, 0, 2))

    expert_range = jnp.arange(groups, dtype=jnp.int32)
    owner = jnp.sum(jnp.where(expert_ids[..., None] == expert_range, owner_map, 0), axis=-1)
    lane = jnp.arange(LANES, dtype=jnp.int32)
    coefficient = jnp.sum(
        jnp.where(owner[..., None] == lane % groups, route_weights[..., None], 0.0), axis=2
    )
    high = lax.reduce_precision(coefficient, 8, 7)
    middle = lax.reduce_precision(coefficient - high, 8, 7)
    low = coefficient - high - middle
    ext = jnp.where(lane < groups, high, jnp.where(lane < 2 * groups, middle, jnp.where(lane < 3 * groups, low, 0.0)))
    ext = ext.astype(jnp.bfloat16)

    routes = (groups - 1) + groups * (copies - 1)
    vmem = pl.BlockSpec(memory_space=pltpu.VMEM)
    dma = pltpu.SemaphoreType.DMA
    return pl.pallas_call(
        functools.partial(kernel, groups, copies),
        out_shape=jax.ShapeDtypeStruct((steps, rows, width), jnp.bfloat16),
        in_specs=[vmem, vmem, pl.BlockSpec(memory_space=pl.ANY)],
        out_specs=vmem,
        scratch_shapes=[
            pltpu.VMEM((3, units, width), jnp.bfloat16),
            pltpu.VMEM((steps, device_count, rows, width + LANES), jnp.bfloat16),
            pltpu.VMEM((steps, groups, copies, rows, width), jnp.bfloat16),
            pltpu.VMEM((steps, copies, groups, rows, width), jnp.bfloat16),
            pltpu.VMEM((steps, groups, rows, width), jnp.bfloat16),
            pltpu.VMEM((steps, groups, rows, width), jnp.bfloat16),
            dma((3,)),
            dma((steps, routes)),
            dma((steps, routes)),
            dma((steps, PIECES, copies - 1)),
            dma((steps, PIECES, copies - 1)),
            dma((steps, PIECES, groups - 1)),
            dma((steps, PIECES, groups - 1)),
        ],
        compiler_params=pltpu.CompilerParams(
            collective_id=0, has_side_effects=True, vmem_limit_bytes=56 * 1024 * 1024
        ),
    )(tokens, ext, weights)


def solution(mesh):
    placed = (
        P(None, ("dp", "expert"), None),
        P(None, ("dp", "expert"), None),
        P(None, ("dp", "expert"), None),
        P("dp"),
        P("expert", None, None),
    )
    return jax.shard_map(
        shards,
        mesh=mesh,
        in_specs=placed,
        out_specs=P(None, ("dp", "expert"), None),
        check_vma=False,
    )
```

time: 120 us -> 64.2 us (0.54)
  waiting for transfers between devices: 70.9 us -> 0 us
  Pallas kernels: 0 us -> 60.2 us
  matrix products: 20.7 us -> 0 us
  starting transfers between devices: 18 us -> 0 us
  local copies, waits for them, and re-layouts: 5.57 us -> 1.64 us
  other arithmetic: 3.64 us -> 2.17 us
    all_to_all x4 -> x0, waiting for transfers between devices: 70.9 us -> none  [the longest x2 35.7 us: cold_path(): lax.all_to_all(outgoing, 'expert', split_axis=0, concat_axis=0, tiled=True)]
    pallas_call x0 -> x1, Pallas kernels: none -> 60.2 us  [shards(): pl.pallas_call(functools.partial(kernel, groups, copies), out_shape=jax.S...]
    dot_general x6 -> x0, matrix products: 20.7 us -> none  [the longest x2 11 us: expert_apply(): jnp.einsum('nd,hgd->ngh', tok_rows, weights[:, :2, :], preferred_element_...]
    all_to_all x4 -> x0, starting transfers between devices: 18 us -> none  [the longest x2 10.8 us: cold_path(): lax.all_to_all(outgoing, 'expert', split_axis=0, concat_axis=0, tiled=True)]
    broadcast_in_dim x2 -> x0, local copies, waits for them, and re-layouts: 2.02 us -> none  [cold_path(): jnp.broadcast_to(blocks[:, None], (EXPERTS, copies, capacity, width))]
    unnamed x4 -> x1, local copies, waits for them, and re-layouts: 0.01 us -> 1.64 us
    gather x2 -> x0, local copies, waits for them, and re-layouts: 1.42 us -> none  [cold_path(): jnp.take(summed, flat_index.reshape(-1), axis=0)]
  transfers between devices with their start and end apart: 4 -> 0, of which waited for: 4 -> 0; matrix products, arithmetic and copies ran while one was open for 18% -> 0% of each run, Pallas kernels for 0% -> 0%
where the time goes in v1:
time: 64.2 us; the launch traced here: 64 us
  Pallas kernels  60.2 us (94%)
  other arithmetic  2.17 us (3%)
  local copies, waits for them, and re-layouts  1.64 us (3%)
    pallas_call x1, Pallas kernels, shards(): pl.pallas_call(functools.partial(kernel, groups, copies), out_shape=jax.S...  60.2 us
    unnamed x1, local copies, waits for them, and re-layouts  1.64 us

profile of v1, /device:TPU:0, one launch (start us, length us, event | category | flops | bytes accessed | tf_op | source)
XLA Modules:
  0.0 64.0 jit_solution(16762753161361865941)
XLA Ops:
  0.0 0.8 %select_reduce_fusion.1 = s32[2,16,2]{1,2,0:T(2,128)S(1)} fusion(s32[4]{0:T(128)} %param.8, s32[2,16,2]{1,2,0:T(2,128)} %param.6), kind=kLoop, calls=%fused_computation.7 | loop fusion | flops 704 | bytes 528 | tf_op jit(solution)/shard_map/reduce_sum | solution.py:175
  0.8 0.8 %select_reduce_fusion = f32[2,16,128]{2,1,0:T(8,128)S(1)} fusion(f32[2,16,2]{1,2,0:T(2,128)} %param.7, s32[128]{0:T(128)S(1)} %and_select_fusion, s32[2,16,2]{1,2,0:T(2,128)S(1)} %select_reduce_fusion.1), kind=kLoop, calls=%fused_computation | loop fusion | flops 20480 | bytes 17408 | tf_op jit(solution)/shard_map/reduce_sum | solution.py:177
  1.6 0.6 fusion.ext_ref
  2.2 60.2 %shard_map.55 = bf16[2,16,3584]{2,1,0:T(8,128)(2,1)} custom-call(bf16[2,16,3584]{2,1,0:T(8,128)(2,1)} %x_ref.1, bf16[2,16,128]{2,1,0:T(8,128)(2,1)} %fusion.ext_ref, bf16[3,512,3584]{2,1,0:T(8,128)(2,1)} %bitcast.1), custom_call_target="tpu_custom_call" | custom-call | tf_op jit(solution)/shard_map/pallas_call | solution.py:189
  62.4 1.6 %copy.9 = bf16[2,16,3584]{2,1,0:T(8,128)(2,1)} copy(bf16[2,16,3584]{2,1,0:T(8,128)(2,1)} %shard_map.55) | data formatting | bytes 458752
  (3 shorter events, 0.0 us)

commit v2 on v1

--- a/solution.py
+++ b/solution.py
@@ -8,10 +8,29 @@
 from jax.sharding import PartitionSpec as P
 
 LANES = 128
-PIECES = 2
-
-
-def kernel(groups, copies, x_ref, ext_ref, w_ref, out_ref, w_buf, got, part, from_minor, joined, from_major,
+PIECES = 4
+
+
+def coefficients(groups, rows, ids, route, owner_ref):
+    diagonal = lax.broadcasted_iota(jnp.int32, (rows, rows), 0) == lax.broadcasted_iota(jnp.int32, (rows, rows), 1)
+    lane = lax.broadcasted_iota(jnp.int32, (rows, LANES), 1)
+    group = (lane % groups).astype(jnp.float32)
+    total = jnp.zeros((rows, LANES), jnp.float32)
+    for k in range(ids.shape[0]):
+        owner = jnp.zeros((1, rows), jnp.float32)
+        for e in range(groups):
+            owner += jnp.where(ids[k:k + 1] == e, owner_ref[e].astype(jnp.float32), 0.0)
+        owner = jnp.sum(jnp.where(diagonal, owner, 0.0), axis=1, keepdims=True)
+        weight = jnp.sum(jnp.where(diagonal, route[k:k + 1], 0.0), axis=1, keepdims=True)
+        total += jnp.where(owner == group, weight, 0.0)
+    high = total.astype(jnp.bfloat16).astype(jnp.float32)
+    middle = (total - high).astype(jnp.bfloat16).astype(jnp.float32)
+    low = total - high - middle
+    ext = jnp.where(lane < groups, high, jnp.where(lane < 2 * groups, middle, jnp.where(lane < 3 * groups, low, 0.0)))
+    return ext.astype(jnp.bfloat16)
+
+
+def kernel(groups, copies, x_ref, ids_ref, route_ref, owner_ref, w_ref, out_ref, w_buf, got, part, from_minor, joined, from_major,
            w_sem, gs_sem, gr_sem, ms_sem, mr_sem, zs_sem, zr_sem):
     steps, rows, width = x_ref.shape
     units = w_ref.shape[1]
@@ -27,7 +46,7 @@
         load.start()
     for s in range(steps):
         got[s, me, :, :width] = x_ref[s]
-        got[s, me, :, width:] = ext_ref[s]
+        got[s, me, :, width:] = coefficients(groups, rows, ids_ref[s], route_ref[s], owner_ref)
 
     barrier = pltpu.get_barrier_semaphore()
     for mp in majors:
@@ -171,25 +190,13 @@
     units = expert_weights.shape[0]
     weights = jnp.transpose(expert_weights, (1, 0, 2))
 
-    expert_range = jnp.arange(groups, dtype=jnp.int32)
-    owner = jnp.sum(jnp.where(expert_ids[..., None] == expert_range, owner_map, 0), axis=-1)
-    lane = jnp.arange(LANES, dtype=jnp.int32)
-    coefficient = jnp.sum(
-        jnp.where(owner[..., None] == lane % groups, route_weights[..., None], 0.0), axis=2
-    )
-    high = lax.reduce_precision(coefficient, 8, 7)
-    middle = lax.reduce_precision(coefficient - high, 8, 7)
-    low = coefficient - high - middle
-    ext = jnp.where(lane < groups, high, jnp.where(lane < 2 * groups, middle, jnp.where(lane < 3 * groups, low, 0.0)))
-    ext = ext.astype(jnp.bfloat16)
-
     routes = (groups - 1) + groups * (copies - 1)
     vmem = pl.BlockSpec(memory_space=pltpu.VMEM)
     dma = pltpu.SemaphoreType.DMA
     return pl.pallas_call(
         functools.partial(kernel, groups, copies),
         out_shape=jax.ShapeDtypeStruct((steps, rows, width), jnp.bfloat16),
-        in_specs=[vmem, vmem, pl.BlockSpec(memory_space=pl.ANY)],
+        in_specs=[vmem, vmem, vmem, pl.BlockSpec(memory_space=pltpu.SMEM), pl.BlockSpec(memory_space=pl.ANY)],
         out_specs=vmem,
         scratch_shapes=[
             pltpu.VMEM((3, units, width), jnp.bfloat16),
@@ -209,7 +216,9 @@
         compiler_params=pltpu.CompilerParams(
             collective_id=0, has_side_effects=True, vmem_limit_bytes=56 * 1024 * 1024
         ),
-    )(tokens, ext, weights)
+    )(
+        tokens, jnp.transpose(expert_ids, (0, 2, 1)), jnp.transpose(route_weights, (0, 2, 1)), owner_map, weights
+    )
 
 
 def solution(mesh):

time: 64.2 us -> 60.8 us (0.947)
  other arithmetic: 2.17 us -> 0 us
  Pallas kernels: 60.2 us -> 59 us
    reduce_sum x2 -> x0, other arithmetic: 1.54 us -> none  [the longest x1 0.78 us: shards(): jnp.sum(jnp.where(expert_ids[..., None] == expert_range, owner_map, 0), a...]
    pallas_call x1, Pallas kernels: 60.2 us -> 59 us  [shards(): pl.pallas_call(functools.partial(kernel, groups, copies), out_shape=jax.S...]
where the time goes in v2:
time: 60.8 us; the launch traced here: 60.7 us
  Pallas kernels  59 us (97%)
  local copies, waits for them, and re-layouts  1.64 us (3%)
    pallas_call x1, Pallas kernels, shards(): pl.pallas_call(functools.partial(kernel, groups, copies), out_shape=jax.S...  59 us
    unnamed x1, local copies, waits for them, and re-layouts  1.64 us

profile of v2, /device:TPU:0, one launch (start us, length us, event | category | flops | bytes accessed | tf_op | source)
XLA Modules:
  0.0 60.7 jit_solution(282615249461806905)
XLA Ops:
  0.0 59.0 %shard_map.55 = bf16[2,16,3584]{2,1,0:T(8,128)(2,1)} custom-call(bf16[2,16,3584]{2,1,0:T(8,128)(2,1)} %x_ref.1, s32[2,2,16]{2,1,0:T(2,128)} %bitcast.4, f32[2,2,16]{2,1,0:T(2,128)} %bitcast.5, s32[4]{0:T(128)} %owner_ref.1, bf16[3,512,3584]{2,1,0:T(8,128)(2,1)} %bitcast.3), custom_call_target="tpu_custom_call" | custom-call | tf_op jit(solution)/shard_map/pallas_call | solution.py:196
  59.0 1.6 %copy.7 = bf16[2,16,3584]{2,1,0:T(8,128)(2,1)} copy(bf16[2,16,3584]{2,1,0:T(8,128)(2,1)} %shard_map.55) | data formatting | bytes 458752
